TPU v7x, 32 devices: a whole 2x2x4 slice. The times are simulated.
32 devices in a mesh: gx: 8 (over y, x, core), gy: 4 (over z).
Axes of the slice: x: 2, y: 2, z: 4, core: 2. Of those that a mesh axis runs over, the one named last changes fastest.
Arguments:
- features: bfloat16 [32768, 256], P(('gx', 'gy')), may hold values from -6 to 6
- valid: int32 [32768], P(('gx', 'gy')), may hold values from 0 to 1, as said below
- cotangent: bfloat16 [32768, 256], P(('gx', 'gy')), may hold values from -6 to 6
- gamma: float32 [256], replicated, may hold values from 0.5 to 1.5
- w_qkv: bfloat16 [256, 768], replicated
- w_out: bfloat16 [256, 256], replicated, may hold values from -0.375 to 0.375
Outputs:
- block_out: bfloat16 [32768, 256], P(('gx', 'gy'))
- grad_x: bfloat16 [32768, 256], P(('gx', 'gy'))
- grad_wqkv: float32 [256, 768], replicated
- grad_wout: float32 [256, 256], replicated
- gamma_gradient: float32 [256], replicated
Inputs may be any that keep to these rules, and one draw needn't show every extreme that they name: `valid`: the node that takes the first position of each patch in transposed order is occupied.
All inputs are finite; a program needn't handle non-finite values.
Results may differ from a plain program's by a relative error of at most 0.015.
The roundings to bfloat16 on the way count: a program that leaves them out, or rounds other values in their place, can miss the bound.
Values may be sent and summed in bfloat16 or wider, within the bound.
A program may use at most 64 MiB of HBM per device.

v0:
```python
import jax
import jax.numpy as jnp
from jax import lax
from jax.sharding import PartitionSpec as P

HEADS = 16
K = 1024


def layer_norm_apply(input_rows, gamma):
    xf = input_rows.astype(jnp.float32)
    centered_input = xf - jnp.mean(xf, -1, keepdims=True)
    reciprocal_deviation = lax.rsqrt(
        jnp.mean(centered_input * centered_input, -1, keepdims=True) + 1e-05
    )
    normalized_input = centered_input * reciprocal_deviation
    return (normalized_input, reciprocal_deviation, (normalized_input * gamma).astype(jnp.bfloat16))


def head_probs(query, keys, keep, scale):
    scores = jnp.dot(query, keys.T, preferred_element_type=jnp.float32) * scale
    scores = jnp.where(keep[None, :], scores, -1e30)
    expo = jnp.exp(scores - jnp.max(scores, -1, keepdims=True))
    return expo / jnp.sum(expo, -1, keepdims=True)


def split_heads(block, heads):
    return block.reshape(block.shape[0], heads, -1).transpose(1, 0, 2)


def join_heads(block):
    return block.transpose(1, 0, 2).reshape(block.shape[1], -1)


def patch_forward(qkv_block, keep, heads):
    width = qkv_block.shape[1] // 3
    scale = (width // heads) ** (-0.5)
    query = split_heads(qkv_block[:, :width], heads)
    keys = split_heads(qkv_block[:, width : 2 * width], heads)
    values = split_heads(qkv_block[:, 2 * width :], heads)

    def one_head(parts):
        probs = head_probs(parts[0], parts[1], keep, scale).astype(jnp.bfloat16)
        return jnp.dot(probs, parts[2], preferred_element_type=jnp.float32).astype(jnp.bfloat16)

    return join_heads(lax.map(one_head, (query, keys, values)))


def patch_backward(qkv_block, keep, grad_block, heads):
    width = qkv_block.shape[1] // 3
    scale = (width // heads) ** (-0.5)
    query = split_heads(qkv_block[:, :width], heads)
    keys = split_heads(qkv_block[:, width : 2 * width], heads)
    values = split_heads(qkv_block[:, 2 * width :], heads)
    grads = split_heads(grad_block, heads)

    def one_head(parts):
        q_head, k_head, v_head, g_head = parts
        probs = head_probs(q_head, k_head, keep, scale)
        rounded = probs.astype(jnp.bfloat16)
        d_value = jnp.dot(rounded.T, g_head, preferred_element_type=jnp.float32).astype(
            jnp.bfloat16
        )
        d_prob = jnp.dot(g_head, v_head.T, preferred_element_type=jnp.float32)
        d_score = (probs * (d_prob - jnp.sum(d_prob * probs, -1, keepdims=True)) * scale).astype(
            jnp.bfloat16
        )
        d_query = jnp.dot(d_score, k_head, preferred_element_type=jnp.float32).astype(jnp.bfloat16)
        d_key = jnp.dot(d_score.T, q_head, preferred_element_type=jnp.float32).astype(jnp.bfloat16)
        return (d_query, d_key, d_value)

    d_query, d_key, d_value = lax.map(one_head, (query, keys, values, grads))
    return jnp.concatenate([join_heads(d_query), join_heads(d_key), join_heads(d_value)], 1)


def relayout_pair(first, second):
    size_x = lax.axis_size("gx")
    size_y = lax.axis_size("gy")
    first_s = first.reshape(size_x * size_y, -1, first.shape[1])
    second_s = second.reshape(size_x * size_y, -1)
    moved_a, moved_b = (
        lax.all_to_all(first_s, ("gx", "gy"), split_axis=0, concat_axis=0, tiled=True),
        lax.all_to_all(second_s, ("gx", "gy"), split_axis=0, concat_axis=0, tiled=True),
    )
    return (moved_a.reshape(first.shape), moved_b.reshape(second.shape))


def relayout_one(array):
    size_x = lax.axis_size("gx")
    size_y = lax.axis_size("gy")
    shaped = array.reshape(size_x * size_y, -1, array.shape[1])
    moved = lax.all_to_all(shaped, ("gx", "gy"), split_axis=0, concat_axis=0, tiled=True)
    return moved.reshape(array.shape)


def shards(features, valid, cotangent, gamma, w_qkv, w_out):
    rows, width = features.shape
    patches = rows // K
    nodes = rows * lax.axis_size("gx") * lax.axis_size("gy")
    inverse_root = float(nodes) ** (-0.5)
    input_rows, occupied = relayout_pair(features, valid.astype(jnp.bfloat16))
    keep = occupied > 0.5
    normalized_input, reciprocal_deviation, hidden_state = layer_norm_apply(input_rows, gamma)
    qkv = jnp.dot(hidden_state, w_qkv, preferred_element_type=jnp.float32).astype(jnp.bfloat16)
    qkv_p = qkv.reshape(patches, K, 3 * width)
    keep_p = keep.reshape(patches, K)
    attn = lax.map(lambda a: patch_forward(a[0], a[1], HEADS), (qkv_p, keep_p)).reshape(rows, width)
    y_val = (
        input_rows.astype(jnp.float32) + jnp.dot(attn, w_out, preferred_element_type=jnp.float32)
    ).astype(jnp.bfloat16)
    y_plain = relayout_one(y_val)
    gt = relayout_one(cotangent)
    local_wout = jnp.dot(attn.T, gt, preferred_element_type=jnp.float32)
    d_attn = jnp.dot(gt, w_out.T, preferred_element_type=jnp.float32).astype(jnp.bfloat16)
    d_attn_p = d_attn.reshape(patches, K, width)
    d_qkv = lax.map(
        lambda a: patch_backward(a[0], a[1], a[2], HEADS), (qkv_p, keep_p, d_attn_p)
    ).reshape(rows, 3 * width)
    local_wqkv = jnp.dot(hidden_state.T, d_qkv, preferred_element_type=jnp.float32)
    hidden_gradient = jnp.dot(d_qkv, w_qkv.T, preferred_element_type=jnp.float32)
    shard_gamma = jnp.sum(hidden_gradient * normalized_input, 0)
    scaled_output = hidden_gradient * gamma
    norm_gradient = reciprocal_deviation * (
        scaled_output
        - jnp.mean(scaled_output, -1, keepdims=True)
        - normalized_input * jnp.mean(scaled_output * normalized_input, -1, keepdims=True)
    )
    d_x = (gt.astype(jnp.float32) + norm_gradient).astype(jnp.bfloat16)
    total_wqkv, total_wout, total_gamma = lax.psum(
        (local_wqkv, local_wout, shard_gamma), ("gx", "gy")
    )
    dx_plain = relayout_one(d_x)
    return (
        y_plain,
        dx_plain,
        total_wqkv * inverse_root,
        total_wout * inverse_root,
        total_gamma * inverse_root,
    )


def solution(mesh):
    placed = (P(("gx", "gy"), None), P(("gx", "gy")), P(("gx", "gy"), None), P(), P(), P())
    return jax.shard_map(
        shards,
        mesh=mesh,
        in_specs=placed,
        out_specs=(P(("gx", "gy"), None), P(("gx", "gy"), None), P(), P(), P()),
        check_vma=False,
    )
```

profile of v0, /device:TPU:0, one launch (start us, length us, event | category | flops | bytes accessed | tf_op | source)
XLA Modules:
  0.0 462.9 jit_solution(17087111885266508579)
XLA Ops:
  8.0 14.3 %all_to_all.30 = bf16[32,1,32]{2,1,0:T(2,128)(2,1)S(1)} all-to-all(bf16[32,1,32]{2,1,0:T(2,128)(2,1)S(1)} %all_to_all.24), channel_id=1, replica_groups=mesh['gx'=8,'gy'=4] {'gx','gy'}, dimensions={0} | all-to-all | bytes 4096 | tf_op jit(solution)/shard_map/all_to_all | solution.py:83
  25.0 14.2 %all-to-all-done = bf16[32,32,256]{2,1,0:T(8,128)(2,1)S(1)} async-done(((bf16[32,32,256]{2,1,0:T(8,128)(2,1)}), bf16[32,32,256]{2,1,0:T(8,128)(2,1)S(1)}, u32[]{:S(2)}, u32[]{:S(2)}) %all-to-all-start) | async-done | bytes 524320 | tf_op jit(solution)/shard_map/all_to_all | solution.py:82
  39.3 4.0 all-to-all-start.3
  46.7 11.0 %all-to-all-done.3 = bf16[32,32,256]{2,1,0:T(8,128)(2,1)S(1)} async-done(((bf16[32,32,256]{2,1,0:T(8,128)(2,1)}), bf16[32,32,256]{2,1,0:T(8,128)(2,1)S(1)}, u32[]{:S(2)}, u32[]{:S(2)}) %all-to-all-start.3) | async-done | bytes 524320 | tf_op jit(solution)/shard_map/all_to_all | solution.py:92
  61.4 172.3 %while.41 = (s32[]{:T(128)}, bf16[16,1024,16]{1,2,0:T(8,128)(2,1)}, bf16[16,1024,16]{1,2,0:T(8,128)(2,1)}, bf16[16,1024,16]{1,2,0:T(8,128)(2,1)}, pred[1024]{0:T...) while((s32[]{:T(128)}, bf16[16,1024,16]{1,2,0:T(8,128)(2,1)}, ...), condition=%wide.region_10.11_spmd, body=%wide.region_6.10_spmd.sunk | while | flops 195081216 | bytes 36034660 | solution.py:72
  63.1 2.6 fusion.106
  73.9 2.6 fusion.106
  84.7 2.6 fusion.106
  95.4 2.6 fusion.106
  117.0 2.7 fusion.106
  138.5 2.6 fusion.106
  170.8 2.6 fusion.106
  181.6 2.6 fusion.106
  192.3 2.6 fusion.106
  203.1 2.6 fusion.106
  213.9 2.6 fusion.106
  224.6 2.6 fusion.106
  233.7 2.8 multiply_reduce_fusion.1
  238.2 4.1 all-to-all-start.4
  242.6 70.3 %while.40 = (s32[]{:T(128)}, bf16[16,1024,16]{1,2,0:T(8,128)(2,1)S(1)}, pred[1024]{0:T(1024)(128)(4,1)S(1)}, bf16[16,1024,16]{1,2,0:T(8,128)(2,1)}, bf16[16,1024...) while((s32[]{:T(128)}, bf16[16,1024,16]{1,2,0:T(8,128)(2,1)S(1)}, ...), condition=%wide.region_5.6_spmd, body=%wide.region_2.5_spmd.sunk | while | flops 79706112 | bytes 12739661 | solution.py:46
  313.9 2.9 fusion.59
  318.0 5.8 %all-to-all-start.2 = ((bf16[32,32,256]{2,1,0:T(8,128)(2,1)}), bf16[32,32,256]{2,1,0:T(8,128)(2,1)S(1)}, u32[]{:S(2)}, u32[]{:S(2)}) async-start(bf16[32,32,256]{2,1,0:T(8,128)(2,1)} %bitcast.21), calls=%async_computation.2 | async-start | bytes 1048576 | tf_op jit(solution)/shard_map/all_to_all | solution.py:92
  323.8 41.4 %psum.23 = f32[256]{0:T(256)S(1)} all-reduce(f32[256]{0:T(256)S(1)} %get-tuple-element.117), channel_id=1, replica_groups=mesh['gx'=8,'gy'=4] {'gx','gy'}, use_global_device_ids=true, to_apply=%region_16.17 | all-reduce | flops 256 | bytes 2048 | tf_op jit(solution)/shard_map/psum | solution.py:129
  365.7 84.9 %all-reduce.3.cloned.1.call-done = (f32[256,768]{1,0:T(8,128)}, f32[256,256]{1,0:T(8,128)}) async-done(((f32[256,768]{1,0:T(8,128)}, f32[256,256]{1,0:T(8,128)}), (f32[256,768]{1,0:T(8,128)}, f32[256,256]{1,0:T(8,128)})) %all-reduce.3.cloned.1.call-update) | async-done | bytes 1048592 | tf_op jit(solution)/shard_map/psum | solution.py:129
  (190 shorter events, 230.7 us)
Async XLA Ops:
  7.2 38.0 %copy-start = (bf16[256,768]{1,0:T(8,128)(2,1)S(1)}, bf16[256,768]{1,0:T(8,128)(2,1)}, u32[]{:S(2)}) copy-start(bf16[256,768]{1,0:T(8,128)(2,1)} %param.14) | copy-start | bytes 1179652
  22.3 17.0 %all-to-all-start = ((bf16[32,32,256]{2,1,0:T(8,128)(2,1)}), bf16[32,32,256]{2,1,0:T(8,128)(2,1)S(1)}, u32[]{:S(2)}, u32[]{:S(2)}) async-start(bf16[32,32,256]{2,1,0:T(8,128)(2,1)} %bitcast.155), calls=%async_computation | async-start | bytes 1048576 | tf_op jit(solution)/shard_map/all_to_all | solution.py:82
  39.3 18.4 %all-to-all-start.3 = ((bf16[32,32,256]{2,1,0:T(8,128)(2,1)}), bf16[32,32,256]{2,1,0:T(8,128)(2,1)S(1)}, u32[]{:S(2)}, u32[]{:S(2)}) async-start(bf16[32,32,256]{2,1,0:T(8,128)(2,1)} %bitcast.156), calls=%async_computation.3 | async-start | bytes 1048576 | tf_op jit(solution)/shard_map/all_to_all | solution.py:92
  43.3 14.4 %copy-start.2 = (bf16[256,256]{1,0:T(8,128)(2,1)S(1)}, bf16[256,256]{1,0:T(8,128)(2,1)}, u32[]{:S(2)}) copy-start(bf16[256,256]{1,0:T(8,128)(2,1)} %param.15) | copy-start | bytes 393220
  61.4 172.3 %copy-start.4 = (f32[256]{0:T(256)S(1)}, f32[256]{0:T(256)}, u32[]{:S(2)}) copy-start(f32[256]{0:T(256)} %param.13) | copy-start | bytes 3076
  233.7 4.5 copy-start.1
  238.2 79.8 %all-to-all-start.4 = ((bf16[32,32,256]{2,1,0:T(8,128)(2,1)}), bf16[32,32,256]{2,1,0:T(8,128)(2,1)S(1)}, u32[]{:S(2)}, u32[]{:S(2)}) async-start(bf16[32,32,256]{2,1,0:T(8,128)(2,1)} %bitcast.36), calls=%async_computation.4 | async-start | bytes 1048576 | tf_op jit(solution)/shard_map/all_to_all | solution.py:92
  242.3 208.4 %all-reduce.3.cloned.1.call-start = ((), (), s32[]{:S(2)}) async-start(), calls=%async_computation.5 | async-start | bytes 2097152 | tf_op jit(solution)/shard_map/psum | solution.py:129
  312.9 3.9 copy-start.3
  318.0 136.5 %all-to-all-start.2 = ((bf16[32,32,256]{2,1,0:T(8,128)(2,1)}), bf16[32,32,256]{2,1,0:T(8,128)(2,1)S(1)}, u32[]{:S(2)}, u32[]{:S(2)}) async-start(bf16[32,32,256]{2,1,0:T(8,128)(2,1)} %bitcast.21), calls=%async_computation.2 | async-start | bytes 1048576 | tf_op jit(solution)/shard_map/all_to_all | solution.py:92
Sparse Core Ops, SparseCore 0:
  316.9 133.7 all-reduce.2
where the time goes:
time: 468 us; the launch traced here: 463 us
  matrix products  193 us (41%)
  waiting for transfers between devices  110 us (24%)
  other arithmetic  67.1 us (14%)
  blocking collectives  55.6 us (12%)
  starting transfers between devices  16.8 us (4%)
  between operations  14.2 us (3%)
  local copies, waits for them, and re-layouts  5.49 us (1%)
    psum x1, waiting for transfers between devices, shards(): lax.psum((local_wqkv, local_wout, shard_gamma), ('gx', 'gy'))  84.9 us
    dot_general x16, matrix products, one_head(): jnp.dot(rounded.T, g_head, preferred_element_type=jnp.float32)  42.3 us
    psum x1, blocking collectives, shards(): lax.psum((local_wqkv, local_wout, shard_gamma), ('gx', 'gy'))  41.4 us
    dot_general x32, matrix products, head_probs(): scores = jnp.dot(query, keys.T, preferred_element_type=jnp.float32) * scale  37.5 us
    dot_general x16, matrix products, one_head(): d_prob = jnp.dot(g_head, v_head.T, preferred_element_type=jnp.float32)  35.9 us
    dot_general x16, matrix products, one_head(): jnp.dot(probs, parts[2], preferred_element_type=jnp.float32)  30.7 us
    convert_element_type x16, other arithmetic, one_head(): (probs * (d_prob - jnp.sum(d_prob * probs, -1, keepdims=True)) * scale).a...  29.6 us
    reduce_sum x32, other arithmetic, head_probs(): return expo / jnp.sum(expo, -1, keepdims=True)  29.1 us
  transfers between devices with their start and end apart: 5, of which 3 were waited for; matrix products, arithmetic and copies ran while one was open for 18% of the time, Pallas kernels for 0%

commit v1 on v0

v1 whole, which is shorter than its diff:
```python
import functools

import jax
import jax.numpy as jnp
from jax import lax
from jax.experimental import pallas as pl
from jax.experimental.pallas import tpu as pltpu
from jax.sharding import PartitionSpec as P

HEADS = 16
K = 1024
QB = 256
MESH = pl.DeviceIdType.MESH
BF = jnp.bfloat16
F32 = jnp.float32
LOG2E = 1.4426950408889634
LIMIT = 56 * 1024 * 1024


def nn(a, b):
    return jnp.dot(a, b, preferred_element_type=F32)


def nt(a, b):
    return lax.dot_general(a, b, (((1,), (1,)), ((), ())), preferred_element_type=F32)


def place(sizes):
    nx, ny = sizes
    n = nx * ny
    me = lax.axis_index("gx") * ny + lax.axis_index("gy")
    return n, ny, me


def enter(sizes):
    n, ny, me = place(sizes)
    barrier = pltpu.get_barrier_semaphore()

    def body(i, c):
        t = lax.rem(me + i, n)
        pl.semaphore_signal(barrier, inc=1, device_id=(t // ny, lax.rem(t, ny)), device_id_type=MESH)
        return c

    lax.fori_loop(1, n, body, 0)
    pl.semaphore_wait(barrier, n - 1)


def exchange(sizes, src, dst, send, recv, one=False):
    n, ny, me = place(sizes)

    def copy(i):
        t = lax.rem(me + i, n)
        return t, pltpu.make_async_remote_copy(
            src_ref=src(t), dst_ref=dst(me), send_sem=send.at[t], recv_sem=recv.at[me],
            device_id=(t // ny, lax.rem(t, ny)), device_id_type=MESH)

    def start(i, c):
        copy(i)[1].start()
        return c

    lax.fori_loop(1, n, start, 0)


def finish(sizes, src, dst, send, recv):
    n, ny, me = place(sizes)

    def wait(i, c):
        t = lax.rem(me + i, n)
        s = lax.rem(me + n - i, n)
        pltpu.make_async_remote_copy(
            src_ref=src(t), dst_ref=dst(s), send_sem=send.at[t], recv_sem=recv.at[s],
            device_id=(t // ny, lax.rem(t, ny)), device_id_type=MESH).wait()
        return c

    lax.fori_loop(1, n, wait, 0)


def rows_of(ref, block):
    return lambda t: ref.at[pl.ds(pl.multiple_of(t * block, block), block), :]


def tile_of(ref):
    return lambda t: ref.at[t]


def inward_kernel(sizes, f_ref, c_ref, v_ref, fo_ref, co_ref, vo_ref, send, recv):
    n, ny, me = place(sizes)
    block = f_ref.shape[0] // n
    pairs = [
        (rows_of(f_ref, block), rows_of(fo_ref, block)),
        (tile_of(v_ref), tile_of(vo_ref)),
        (rows_of(c_ref, block), rows_of(co_ref, block)),
    ]
    enter(sizes)
    for k, (s, d) in enumerate(pairs):
        exchange(sizes, s, d, send.at[k], recv.at[k])
    own = pl.ds(pl.multiple_of(me * block, block), block)
    fo_ref[own, :] = f_ref[own, :]
    co_ref[own, :] = c_ref[own, :]
    vo_ref[me] = v_ref[me]
    for k, (s, d) in enumerate(pairs):
        finish(sizes, s, d, send.at[k], recv.at[k])


def outward_kernel(sizes, root, y_ref, x_ref, g_ref, yo_ref, xo_ref, gw_ref, gwo_ref, gg_ref,
                   got, mine, parts, send, recv):
    n, ny, me = place(sizes)
    block = y_ref.shape[0] // n
    width = parts.shape[2]
    pairs = [
        (tile_of(g_ref), tile_of(got)),
        (rows_of(y_ref, block), rows_of(yo_ref, block)),
        (rows_of(x_ref, block), rows_of(xo_ref, block)),
        (lambda t: mine, tile_of(parts)),
    ]
    enter(sizes)
    for k in range(3):
        s, d = pairs[k]
        exchange(sizes, s, d, send.at[k], recv.at[k])
    own = pl.ds(pl.multiple_of(me * block, block), block)
    yo_ref[own, :] = y_ref[own, :]
    xo_ref[own, :] = x_ref[own, :]
    got[me] = g_ref[me]
    finish(sizes, *pairs[0], send.at[0], recv.at[0])
    total = jnp.sum(got[...].astype(F32), 0) * root
    mine[...] = total[:, :width].astype(BF)
    exchange(sizes, *pairs[3], send.at[3], recv.at[3])
    extra = total[:, width:]
    gg_ref[:, 0:128] = extra[0:1] + extra[2:3]
    gg_ref[:, 128:256] = extra[1:2] + extra[3:4]
    parts[me] = mine[...]
    finish(sizes, *pairs[3], send.at[3], recv.at[3])
    across = 1024 // width
    for t in range(n):
        r, c = 16 * (t // across), width * (t % across)
        left = max(0, min(width, 768 - c))
        if left:
            gw_ref[r : r + 16, c : c + left] = parts[t, :, :left].astype(F32)
        if left < width:
            c0 = c + left - 768
            gwo_ref[r : r + 16, c0 : c0 + width - left] = parts[t, :, left:].astype(F32)
    for k in (1, 2):
        finish(sizes, *pairs[k], send.at[k], recv.at[k])


def split3(a):
    a1 = a.astype(BF)
    rest = a - a1.astype(F32)
    a2 = rest.astype(BF)
    a3 = (rest - a2.astype(F32)).astype(BF)
    return a1, a2, a3


def patch_kernel(n, x_ref, v_ref, g_ref, gamma_ref, wqkv_ref, wout_ref,
                 y_ref, dx_ref, gout_ref,
                 qkvt, dot_, attnt, dqkvt, hs, mask, acc, gacc, dk_acc, dv_acc):
    patch = pl.program_id(0)
    width = wout_ref.shape[0]
    x = x_ref[...].astype(F32)
    cent = x - jnp.mean(x, -1, keepdims=True)
    rstd = lax.rsqrt(jnp.mean(cent * cent, -1, keepdims=True) + 1e-05)
    gamma = gamma_ref[...]
    hs[...] = (cent * rstd * gamma).astype(BF)
    qkvt[...] = nt(wqkv_ref[...].T, hs[...]).astype(BF)
    dot_[...] = nt(wout_ref[...], g_ref[...]).astype(BF)
    first = lax.broadcasted_iota(jnp.int32, (16, 128), 0)
    for i in range(K // 128):
        per = v_ref.shape[0] // (K // 128)
        row = v_ref[per * i].astype(F32)
        for j in range(1, per):
            row = row + v_ref[per * i + j].astype(F32)
        bias = jnp.where(row > 0.5, 0.0, -1e30)
        mask[:, i * 128 : (i + 1) * 128] = jnp.where(first == 0, bias, 0.0).astype(BF)

    def head(h, carry):
        base = pl.multiple_of(h * 16, 16)
        qt = qkvt[pl.ds(base, 16), :]
        kt = qkvt[pl.ds(pl.multiple_of(width + base, 16), 16), :]
        vt = qkvt[pl.ds(pl.multiple_of(2 * width + base, 16), 16), :]
        q1, q2, q3 = split3(qt.astype(F32) * (0.25 * LOG2E))
        ones = jnp.ones((16, K), BF)
        qa = jnp.concatenate([q1, q2, q3, ones], 0)
        ka = jnp.concatenate([kt, kt, kt, mask[...]], 0).T
        va = jnp.concatenate([vt, ones], 0)
        v2 = jnp.concatenate([vt, vt, ones], 0).T
        rows = lax.broadcasted_iota(jnp.int32, (16, QB), 0)
        for b in range(K // QB):
            cols = slice(b * QB, (b + 1) * QB)
            st = nn(ka, qa[:, cols])
            top = jnp.max(st, 0, keepdims=True)
            e32 = jnp.exp2(st - top)
            e = e32.astype(BF)
            ot = nn(va, e)
            r = 1.0 / ot[16:17]
            o = ot[:16] * r
            attnt[pl.ds(base, 16), cols] = o.astype(BF)
            do = dot_[pl.ds(base, 16), cols].astype(F32)
            delta = jnp.sum(do * o, 0, keepdims=True)
            rs = r * 0.25
            a = do * rs
            a1 = a.astype(BF)
            a2 = (a - a1.astype(F32)).astype(BF)
            b1, b2, b3 = split3(-delta * rs)
            low = jnp.where(
                rows == 0, b1.astype(F32),
                jnp.where(rows == 1, b2.astype(F32), jnp.where(rows == 2, b3.astype(F32), 0.0)),
            ).astype(BF)
            both = jnp.concatenate([a1, a2], 0)
            dt = nn(v2, jnp.concatenate([both, low], 0))
            ds = (e32 * dt).astype(BF)
            dqkvt[pl.ds(base, 16), cols] = nn(kt, ds).astype(BF)
            dk = nt(qt[:, cols], ds)
            dv = nt(both, e)
            if b == 0:
                dk_acc[...] = dk
                dv_acc[...] = dv
            else:
                dk_acc[...] += dk
                dv_acc[...] += dv
        dqkvt[pl.ds(pl.multiple_of(width + base, 16), 16), :] = dk_acc[...].astype(BF)
        dqkvt[pl.ds(pl.multiple_of(2 * width + base, 16), 16), :] = (
            4.0 * (dv_acc[:16] + dv_acc[16:])
        ).astype(BF)
        return carry

    lax.fori_loop(0, HEADS, head, 0)

    x = x_ref[...].astype(F32)
    attn = attnt[...].T
    y_ref[...] = (x + nn(attn, wout_ref[...])).astype(BF)
    local_wout = nn(attnt[...], g_ref[...])
    local_wqkv = nn(dqkvt[...], hs[...]).T
    dh = nt(dqkvt[...].T, wqkv_ref[...])
    cent = x - jnp.mean(x, -1, keepdims=True)
    rstd = lax.rsqrt(jnp.mean(cent * cent, -1, keepdims=True) + 1e-05)
    xhat = cent * rstd
    local_gamma = jnp.sum(dh * xhat, 0, keepdims=True)
    g = dh * gamma
    dx = rstd * (g - jnp.mean(g, -1, keepdims=True) - xhat * jnp.mean(g * xhat, -1, keepdims=True))
    dx_ref[...] = (g_ref[...].astype(F32) + dx).astype(BF)

    @pl.when(patch == 0)
    def _():
        acc[:, :768] = local_wqkv
        acc[:, 768:] = local_wout
        gacc[...] = local_gamma

    @pl.when(patch > 0)
    def _():
        acc[:, :768] += local_wqkv
        acc[:, 768:] += local_wout
        gacc[...] += local_gamma

    @pl.when(patch == pl.num_programs(0) - 1)
    def _():
        w = gout_ref.shape[2] - 128
        across = 1024 // w
        total = gacc[...]
        hi = total.astype(BF).astype(F32)
        lo = total - hi
        rows = lax.broadcasted_iota(jnp.int32, (16, 128), 0)
        extra = jnp.where(
            rows == 0, hi[:, :128],
            jnp.where(rows == 1, hi[:, 128:],
                      jnp.where(rows == 2, lo[:, :128], jnp.where(rows == 3, lo[:, 128:], 0.0))),
        ).astype(BF)
        for t in range(n):
            r, c = 16 * (t // across), w * (t % across)
            gout_ref[t, :, :w] = acc[r : r + 16, c : c + w].astype(BF)
            gout_ref[t, :, w:] = extra


def shards(sizes, features, valid, cotangent, gamma, w_qkv, w_out):
    n = sizes[0] * sizes[1]
    rows, width = features.shape
    patches = rows // K
    block = rows // n
    root = float(rows * n) ** (-0.5)
    me = lax.axis_index("gx") * sizes[1] + lax.axis_index("gy")
    lane = jnp.arange(128, dtype=jnp.int32) // block
    spread = jnp.tile(valid.reshape(n, block), (1, 128 // block))
    spread = jnp.where(lane[None, :] == lax.rem(me, 128 // block), spread, 0).astype(BF)
    spread = jnp.broadcast_to(spread[:, None, :], (n, 16, 128))

    vmem = pl.BlockSpec(memory_space=pltpu.VMEM)
    node = jax.ShapeDtypeStruct((rows, width), BF)
    xt, gt, vt = pl.pallas_call(
        functools.partial(inward_kernel, sizes),
        out_shape=(node, node, jax.ShapeDtypeStruct((n, 16, 128), BF)),
        in_specs=[vmem] * 3,
        out_specs=(vmem,) * 3,
        scratch_shapes=[pltpu.SemaphoreType.DMA((3, n)), pltpu.SemaphoreType.DMA((3, n))],
        compiler_params=pltpu.CompilerParams(collective_id=0, has_side_effects=True, vmem_limit_bytes=LIMIT),
        name="inward",
    )(features, cotangent, spread)

    tile = 16384 // n
    row_spec = pl.BlockSpec((K, width), lambda i: (i, 0))

    def whole(shape):
        return pl.BlockSpec(shape, lambda i: (0,) * len(shape))

    y, dx, grads = pl.pallas_call(
        functools.partial(patch_kernel, n),
        grid=(patches,),
        out_shape=(node, node, jax.ShapeDtypeStruct((n, 16, tile + 128), BF)),
        in_specs=[
            row_spec,
            pl.BlockSpec((K // block, 16, 128), lambda i: (i, 0, 0)),
            row_spec,
            whole((1, width)),
            whole((width, 3 * width)),
            whole((width, width)),
        ],
        out_specs=(row_spec, row_spec, whole((n, 16, tile + 128))),
        scratch_shapes=[
            pltpu.VMEM((3 * width, K), BF),
            pltpu.VMEM((width, K), BF),
            pltpu.VMEM((width, K), BF),
            pltpu.VMEM((3 * width, K), BF),
            pltpu.VMEM((K, width), BF),
            pltpu.VMEM((16, K), BF),
            pltpu.VMEM((width, 4 * width), F32),
            pltpu.VMEM((1, width), F32),
            pltpu.VMEM((16, K), F32),
            pltpu.VMEM((32, K), F32),
        ],
        compiler_params=pltpu.CompilerParams(
            dimension_semantics=("arbitrary",), vmem_limit_bytes=LIMIT),
        name="patch",
    )(xt, vt, gt, gamma.reshape(1, width), w_qkv, w_out)

    y_plain, dx_plain, gw, gwo, gg = pl.pallas_call(
        functools.partial(outward_kernel, sizes, root),
        out_shape=(
            node, node,
            jax.ShapeDtypeStruct((width, 3 * width), F32),
            jax.ShapeDtypeStruct((width, width), F32),
            jax.ShapeDtypeStruct((1, width), F32),
        ),
        in_specs=[vmem] * 3,
        out_specs=(vmem,) * 5,
        scratch_shapes=[
            pltpu.VMEM((n, 16, tile + 128), BF),
            pltpu.VMEM((16, tile), BF),
            pltpu.VMEM((n, 16, tile), BF),
            pltpu.SemaphoreType.DMA((4, n)),
            pltpu.SemaphoreType.DMA((4, n)),
        ],
        compiler_params=pltpu.CompilerParams(collective_id=1, has_side_effects=True, vmem_limit_bytes=LIMIT),
        name="outward",
    )(y, dx, grads)
    return y_plain, dx_plain, gw, gwo, gg.reshape(width)


def solution(mesh):
    sizes = (mesh.shape["gx"], mesh.shape["gy"])
    both = P(("gx", "gy"), None)
    return jax.shard_map(
        functools.partial(shards, sizes),
        mesh=mesh,
        in_specs=(both, P(("gx", "gy")), both, P(), P(), P()),
        out_specs=(both, both, P(), P(), P()),
        check_vma=False,
    )
```

time: 468 us -> 192 us (0.41); the launches traced: 463 us -> 192 us
  matrix products: 193 us -> 0 us
  Pallas kernels: 0 us -> 184 us
  waiting for transfers between devices: 110 us -> 0 us
  other arithmetic: 67.1 us -> 0.02 us
  blocking collectives: 55.6 us -> 0 us
  starting transfers between devices: 16.8 us -> 0 us
  between operations: 14.2 us -> 0.69 us
    dot_general x118 -> x0, matrix products: 193 us -> none  [the longest x16 42.3 us: one_head(): jnp.dot(rounded.T, g_head, preferred_element_type=jnp.float32)]
    pallas_call x0 -> x3, Pallas kernels: none -> 184 us  [the longest x1 87.7 us: shards(): pl.pallas_call(functools.partial(patch_kernel, n), grid=(patches,), out_s...]
    psum x1 -> x0, waiting for transfers between devices: 84.9 us -> none  [shards(): lax.psum((local_wqkv, local_wout, shard_gamma), ('gx', 'gy'))]
    psum x1 -> x0, blocking collectives: 41.4 us -> none  [shards(): lax.psum((local_wqkv, local_wout, shard_gamma), ('gx', 'gy'))]
    convert_element_type x19 -> x1, other arithmetic: 33 us -> 0.01 us  [shards(): jnp.where(lane[None, :] == lax.rem(me, 128 // block), spread, 0).astype(BF)]
    reduce_sum x34 -> x0, other arithmetic: 29.7 us -> none  [the longest x32 29.1 us: head_probs(): return expo / jnp.sum(expo, -1, keepdims=True)]
    all_to_all x4 -> x0, waiting for transfers between devices: 25.2 us -> none  [the longest x1 14.2 us: relayout_pair(): lax.all_to_all(first_s, ('gx', 'gy'), split_axis=0, concat_axis=0, tiled=...]
    all_to_all x4 -> x0, starting transfers between devices: 16.6 us -> none  [the longest x3 14 us: relayout_one(): lax.all_to_all(shaped, ('gx', 'gy'), split_axis=0, concat_axis=0, tiled=T...]
  transfers between devices with their start and end apart: 5 -> 0, of which waited for: 3 -> 0; matrix products, arithmetic and copies ran while one was open for 18% -> 0% of each run, Pallas kernels for 0% -> 0%
where the time goes in v1:
time: 192 us
  Pallas kernels  184 us (96%)
  local copies, waits for them, and re-layouts  7.13 us (4%)
    pallas_call x1, Pallas kernels, shards(): pl.pallas_call(functools.partial(patch_kernel, n), grid=(patches,), out_s...  87.7 us
    pallas_call x1, Pallas kernels, shards(): pl.pallas_call(functools.partial(outward_kernel, sizes, root), out_shape=...  58.9 us
    pallas_call x1, Pallas kernels, shards(): pl.pallas_call(functools.partial(inward_kernel, sizes), out_shape=(node,...  37.6 us
    unnamed x15, local copies, waits for them, and re-layouts  6.28 us

profile of v1, /device:TPU:0, one launch (start us, length us, event | category | flops | bytes accessed | tf_op | source)
XLA Modules:
  0.0 192.0 jit_solution(9262561087717619256)
XLA Ops:
  0.6 0.0 copy-start.3
  0.7 0.7 copy-done.3
  1.3 0.1 tile.10
  1.4 0.1 tile.12
  1.5 0.7 broadcast_in_dim.21.v_ref
  2.2 37.6 %inward.1 = (bf16[1024,256]{1,0:T(8,128)(2,1)}, bf16[1024,256]{1,0:T(8,128)(2,1)}, bf16[32,16,128]{2,1,0:T(8,128)(2,1)}) custom-call(bf16[1024,256]{1,0:T(8,128)(2,1)} %f_ref.1, bf16[1024,256]{1,0:T(8,128)(2,1)} %c_ref.1, bf16[32,16,128]{2,1,0:T(8,128)(2,1)} %broadcast_in_dim.21.v_ref), custom_call_target="tpu_custom_call" | custom-call | tf_op jit(solution)/shard_map/inward/pallas_call | solution.py:287
  39.8 87.7 %patch.1 = (bf16[1024,256]{1,0:T(8,128)(2,1)}, bf16[1024,256]{1,0:T(8,128)(2,1)}, bf16[32,16,640]{2,1,0:T(8,128)(2,1)}) custom-call(bf16[1024,256]{1,0:T(8,128)(2,1)} %get-tuple-element.16.x_ref, bf16[32,16,128]{2,1,0:T(8,128)(2,1)} %get-tuple-element.17.v_ref, bf16[1024,256]{1,0:T(8,128)(2,1)} %get-tuple-element.18.g_ref, f32[1,256]{1,0:T(1,128)} %bitcast.2, ...), custom_call_target="tpu_custom_call" | custom-call | tf_op jit(solution)/shard_map/patch/pallas_call | solution.py:303
  127.4 58.9 %outward.1 = (bf16[1024,256]{1,0:T(8,128)(2,1)}, bf16[1024,256]{1,0:T(8,128)(2,1)}, f32[256,768]{1,0:T(8,128)}, f32[256,256]{1,0:T(8,128)}, f32[1,256]{1,0:T(1,128)}) custom-call(bf16[1024,256]{1,0:T(8,128)(2,1)} %get-tuple-element.19.y_ref, bf16[1024,256]{1,0:T(8,128)(2,1)} %get-tuple-element.20.x_ref, bf16[32,16,640]{2,1,0:T(8,128)(2,1)} %get-tuple-element.21.g_ref), custom_call_target="tpu_custom_call" | custom-call | tf_op jit(solution)/shard_map/outward/pallas_call | solution.py:333
  186.3 0.0 copy-start.1
  186.3 1.9 %copy.16 = bf16[1024,256]{1,0:T(8,128)(2,1)} copy(bf16[1024,256]{1,0:T(8,128)(2,1)} %get-tuple-element.32) | data formatting | bytes 1048576
  188.3 0.0 copy-done.1
  188.3 0.0 copy-start
  188.3 0.8 copy.17
  189.1 0.5 copy-done
  189.6 0.0 copy-start.2
  189.6 0.9 copy.18
  190.5 0.2 copy-done.2
  190.7 0.0 copy-start.4
  190.7 0.7 copy.19
  191.4 0.0 copy-done.4
  191.4 0.6 copy.20
  (3 shorter events, 0.0 us)
Async XLA Ops:
  0.6 0.7 copy-start.3
  186.3 1.9 %copy-start.1 = (bf16[1024,256]{1,0:T(8,128)(2,1)S(1)}, bf16[1024,256]{1,0:T(8,128)(2,1)}, u32[]{:S(2)}) copy-start(bf16[1024,256]{1,0:T(8,128)(2,1)} %get-tuple-element.33) | copy-start | bytes 1572868
  188.3 1.3 copy-start
  189.6 1.1 copy-start.2
  190.7 0.7 copy-start.4

commit v2 on v1

--- a/solution.py
+++ b/solution.py
@@ -9,7 +9,7 @@
 
 HEADS = 16
 K = 1024
-QB = 256
+QB = 1024
 MESH = pl.DeviceIdType.MESH
 BF = jnp.bfloat16
 F32 = jnp.float32
@@ -102,45 +102,83 @@
         finish(sizes, s, d, send.at[k], recv.at[k])
 
 
+def parted(left, right, width):
+    rows = lax.broadcasted_iota(jnp.int32, (16, 128), 0)
+    hi_l, hi_r = left.astype(BF).astype(F32), right.astype(BF).astype(F32)
+    block = jnp.where(
+        rows == 0, hi_l,
+        jnp.where(rows == 1, hi_r,
+                  jnp.where(rows == 2, left - hi_l, jnp.where(rows == 3, right - hi_r, 0.0))),
+    )
+    if width > 128:
+        block = jnp.concatenate([block, jnp.zeros((16, width - 128), F32)], 1)
+    return block.astype(BF)
+
+
 def outward_kernel(sizes, root, y_ref, x_ref, g_ref, yo_ref, xo_ref, gw_ref, gwo_ref, gg_ref,
-                   got, mine, parts, send, recv):
-    n, ny, me = place(sizes)
-    block = y_ref.shape[0] // n
+                   got, half, seen, fine, parts, send, recv, s1, r1, s2, r2, s3, r3):
+    nx, ny = sizes
+    n, _, me = place(sizes)
+    mx, my = lax.axis_index("gx"), lax.axis_index("gy")
+    block = x_ref.shape[0] // n
     width = parts.shape[2]
-    pairs = [
-        (tile_of(g_ref), tile_of(got)),
-        (rows_of(y_ref, block), rows_of(yo_ref, block)),
-        (rows_of(x_ref, block), rows_of(xo_ref, block)),
-        (lambda t: mine, tile_of(parts)),
-    ]
+    body = 16 * ny
+
+    def across(size, mine, src, dst, send, recv, along_x):
+        for i in range(1, size):
+            t = lax.rem(mine + i, size)
+            pltpu.make_async_remote_copy(
+                src_ref=src(t), dst_ref=dst(mine), send_sem=send.at[t], recv_sem=recv.at[mine],
+                device_id=(t, my) if along_x else (mx, t), device_id_type=MESH).start()
+
+    def settle(size, mine, src, dst, send, recv, along_x):
+        for i in range(1, size):
+            t = lax.rem(mine + i, size)
+            s = lax.rem(mine + size - i, size)
+            pltpu.make_async_remote_copy(
+                src_ref=src(t), dst_ref=dst(s), send_sem=send.at[t], recv_sem=recv.at[s],
+                device_id=(t, my) if along_x else (mx, t), device_id_type=MESH).wait()
+
+    first = (nx, mx, tile_of(g_ref), tile_of(got), s1, r1, True)
+    second = (ny, my, lambda t: half, tile_of(seen), s2, r2, False)
+    third = (nx, mx, lambda t: fine, tile_of(parts), s3, r3, True)
+    nodes = [(rows_of(y_ref, block), rows_of(yo_ref, block)), (rows_of(x_ref, block), rows_of(xo_ref, block))]
     enter(sizes)
-    for k in range(3):
-        s, d = pairs[k]
-        exchange(sizes, s, d, send.at[k], recv.at[k])
+    across(*first)
+    for k in range(2):
+        exchange(sizes, *nodes[k], send.at[k], recv.at[k])
     own = pl.ds(pl.multiple_of(me * block, block), block)
     yo_ref[own, :] = y_ref[own, :]
     xo_ref[own, :] = x_ref[own, :]
-    got[me] = g_ref[me]
-    finish(sizes, *pairs[0], send.at[0], recv.at[0])
-    total = jnp.sum(got[...].astype(F32), 0) * root
-    mine[...] = total[:, :width].astype(BF)
-    exchange(sizes, *pairs[3], send.at[3], recv.at[3])
-    extra = total[:, width:]
+    got[mx] = g_ref[mx]
+    settle(*first)
+    total = jnp.sum(got[...].astype(F32), 0)
+    extra = total[body:, :128]
+    half[:body, :] = total[:body].astype(BF)
+    half[body:, :] = parted(extra[0:1] + extra[2:3], extra[1:2] + extra[3:4], width)
+    across(*second)
+    seen[my] = half[...]
+    settle(*second)
+    total = jnp.sum(seen[...].astype(F32), 0) * root
+    fine[...] = total[:body].astype(BF)
+    across(*third)
+    extra = total[body:, :128]
     gg_ref[:, 0:128] = extra[0:1] + extra[2:3]
     gg_ref[:, 128:256] = extra[1:2] + extra[3:4]
-    parts[me] = mine[...]
-    finish(sizes, *pairs[3], send.at[3], recv.at[3])
-    across = 1024 // width
+    parts[mx] = fine[...]
+    settle(*third)
+    side = 1024 // width
     for t in range(n):
-        r, c = 16 * (t // across), width * (t % across)
+        r, c = 16 * (t // side), width * (t % side)
+        r0 = 16 * (t % ny)
         left = max(0, min(width, 768 - c))
         if left:
-            gw_ref[r : r + 16, c : c + left] = parts[t, :, :left].astype(F32)
+            gw_ref[r : r + 16, c : c + left] = parts[t // ny, r0 : r0 + 16, :left].astype(F32)
         if left < width:
             c0 = c + left - 768
-            gwo_ref[r : r + 16, c0 : c0 + width - left] = parts[t, :, left:].astype(F32)
-    for k in (1, 2):
-        finish(sizes, *pairs[k], send.at[k], recv.at[k])
+            gwo_ref[r : r + 16, c0 : c0 + width - left] = parts[t // ny, r0 : r0 + 16, left:].astype(F32)
+    for k in range(2):
+        finish(sizes, *nodes[k], send.at[k], recv.at[k])
 
 
 def split3(a):
@@ -151,7 +189,7 @@
     return a1, a2, a3
 
 
-def patch_kernel(n, x_ref, v_ref, g_ref, gamma_ref, wqkv_ref, wout_ref,
+def patch_kernel(sizes, x_ref, v_ref, g_ref, gamma_ref, wqkv_ref, wout_ref,
                  y_ref, dx_ref, gout_ref,
                  qkvt, dot_, attnt, dqkvt, hs, mask, acc, gacc, dk_acc, dv_acc):
     patch = pl.program_id(0)
@@ -166,9 +204,9 @@
     first = lax.broadcasted_iota(jnp.int32, (16, 128), 0)
     for i in range(K // 128):
         per = v_ref.shape[0] // (K // 128)
-        row = v_ref[per * i].astype(F32)
+        row = v_ref[per * i]
         for j in range(1, per):
-            row = row + v_ref[per * i + j].astype(F32)
+            row = row + v_ref[per * i + j]
         bias = jnp.where(row > 0.5, 0.0, -1e30)
         mask[:, i * 128 : (i + 1) * 128] = jnp.where(first == 0, bias, 0.0).astype(BF)
 
@@ -253,21 +291,17 @@
 
     @pl.when(patch == pl.num_programs(0) - 1)
     def _():
-        w = gout_ref.shape[2] - 128
+        nx, ny = sizes
+        w = gout_ref.shape[2]
         across = 1024 // w
         total = gacc[...]
-        hi = total.astype(BF).astype(F32)
-        lo = total - hi
-        rows = lax.broadcasted_iota(jnp.int32, (16, 128), 0)
-        extra = jnp.where(
-            rows == 0, hi[:, :128],
-            jnp.where(rows == 1, hi[:, 128:],
-                      jnp.where(rows == 2, lo[:, :128], jnp.where(rows == 3, lo[:, 128:], 0.0))),
-        ).astype(BF)
-        for t in range(n):
+        extra = parted(total[:, :128], total[:, 128:], w)
+        for t in range(nx * ny):
             r, c = 16 * (t // across), w * (t % across)
-            gout_ref[t, :, :w] = acc[r : r + 16, c : c + w].astype(BF)
-            gout_ref[t, :, w:] = extra
+            r0 = 16 * (t % ny)
+            gout_ref[t // ny, r0 : r0 + 16, :] = acc[r : r + 16, c : c + w].astype(BF)
+        for t in range(nx):
+            gout_ref[t, 16 * ny :, :] = extra
 
 
 def shards(sizes, features, valid, cotangent, gamma, w_qkv, w_out):
@@ -279,14 +313,13 @@
     me = lax.axis_index("gx") * sizes[1] + lax.axis_index("gy")
     lane = jnp.arange(128, dtype=jnp.int32) // block
     spread = jnp.tile(valid.reshape(n, block), (1, 128 // block))
-    spread = jnp.where(lane[None, :] == lax.rem(me, 128 // block), spread, 0).astype(BF)
-    spread = jnp.broadcast_to(spread[:, None, :], (n, 16, 128))
+    spread = jnp.where(lane[None, :] == lax.rem(me, 128 // block), spread, 0).astype(F32)[:, None, :]
 
     vmem = pl.BlockSpec(memory_space=pltpu.VMEM)
     node = jax.ShapeDtypeStruct((rows, width), BF)
     xt, gt, vt = pl.pallas_call(
         functools.partial(inward_kernel, sizes),
-        out_shape=(node, node, jax.ShapeDtypeStruct((n, 16, 128), BF)),
+        out_shape=(node, node, jax.ShapeDtypeStruct((n, 1, 128), F32)),
         in_specs=[vmem] * 3,
         out_specs=(vmem,) * 3,
         scratch_shapes=[pltpu.SemaphoreType.DMA((3, n)), pltpu.SemaphoreType.DMA((3, n))],
@@ -295,24 +328,25 @@
     )(features, cotangent, spread)
 
     tile = 16384 // n
+    nx, ny = sizes
     row_spec = pl.BlockSpec((K, width), lambda i: (i, 0))
 
     def whole(shape):
         return pl.BlockSpec(shape, lambda i: (0,) * len(shape))
 
     y, dx, grads = pl.pallas_call(
-        functools.partial(patch_kernel, n),
+        functools.partial(patch_kernel, sizes),
         grid=(patches,),
-        out_shape=(node, node, jax.ShapeDtypeStruct((n, 16, tile + 128), BF)),
+        out_shape=(node, node, jax.ShapeDtypeStruct((nx, 16 * ny + 16, tile), BF)),
         in_specs=[
             row_spec,
-            pl.BlockSpec((K // block, 16, 128), lambda i: (i, 0, 0)),
+            pl.BlockSpec((K // block, 1, 128), lambda i: (i, 0, 0)),
             row_spec,
             whole((1, width)),
             whole((width, 3 * width)),
             whole((width, width)),
         ],
-        out_specs=(row_spec, row_spec, whole((n, 16, tile + 128))),
+        out_specs=(row_spec, row_spec, whole((nx, 16 * ny + 16, tile))),
         scratch_shapes=[
             pltpu.VMEM((3 * width, K), BF),
             pltpu.VMEM((width, K), BF),
@@ -341,12 +375,14 @@
         in_specs=[vmem] * 3,
         out_specs=(vmem,) * 5,
         scratch_shapes=[
-            pltpu.VMEM((n, 16, tile + 128), BF),
-            pltpu.VMEM((16, tile), BF),
-            pltpu.VMEM((n, 16, tile), BF),
-            pltpu.SemaphoreType.DMA((4, n)),
-            pltpu.SemaphoreType.DMA((4, n)),
-        ],
+            pltpu.VMEM((nx, 16 * ny + 16, tile), BF),
+            pltpu.VMEM((16 * ny + 16, tile), BF),
+            pltpu.VMEM((ny, 16 * ny + 16, tile), BF),
+            pltpu.VMEM((16 * ny, tile), BF),
+            pltpu.VMEM((nx, 16 * ny, tile), BF),
+            pltpu.SemaphoreType.DMA((2, n)),
+            pltpu.SemaphoreType.DMA((2, n)),
+        ] + [pltpu.SemaphoreType.DMA((size,)) for size in (nx, nx, ny, ny, nx, nx)],
         compiler_params=pltpu.CompilerParams(collective_id=1, has_side_effects=True, vmem_limit_bytes=LIMIT),
         name="outward",
     )(y, dx, grads)

time: 192 us -> 147 us (0.77)
  Pallas kernels: 184 us -> 139 us
    pallas_call x1, Pallas kernels: 87.7 us -> 59.7 us  [shards(): pl.pallas_call(functools.partial(patch_kernel, sizes), grid=(patches,), o...]
    pallas_call x1, Pallas kernels: 58.9 us -> 44.6 us  [shards(): pl.pallas_call(functools.partial(outward_kernel, sizes, root), out_shape=...]
    pallas_call x1, Pallas kernels: 37.6 us -> 35 us  [shards(): pl.pallas_call(functools.partial(inward_kernel, sizes), out_shape=(node,...]
where the time goes in v2:
time: 147 us
  Pallas kernels  139 us (95%)
  local copies, waits for them, and re-layouts  5.99 us (4%)
    pallas_call x1, Pallas kernels, shards(): pl.pallas_call(functools.partial(patch_kernel, sizes), grid=(patches,), o...  59.7 us
    pallas_call x1, Pallas kernels, shards(): pl.pallas_call(functools.partial(outward_kernel, sizes, root), out_shape=...  44.6 us
    pallas_call x1, Pallas kernels, shards(): pl.pallas_call(functools.partial(inward_kernel, sizes), out_shape=(node,...  35 us
    unnamed x15, local copies, waits for them, and re-layouts  5.8 us

profile of v2, /device:TPU:0, one launch (start us, length us, event | category | flops | bytes accessed | tf_op | source)
XLA Modules:
  0.0 146.6 jit_solution(11175294770409452760)
XLA Ops:
  0.6 0.0 copy-start.3
  0.7 0.7 copy-done.3
  1.3 0.1 tile.10
  1.4 0.1 tile.12
  1.5 0.6 fusion.v_ref
  2.2 35.0 %inward.1 = (bf16[1024,256]{1,0:T(8,128)(2,1)}, bf16[1024,256]{1,0:T(8,128)(2,1)}, f32[32,1,128]{2,1,0:T(1,128)}) custom-call(bf16[1024,256]{1,0:T(8,128)(2,1)} %f_ref.1, bf16[1024,256]{1,0:T(8,128)(2,1)} %c_ref.1, f32[32,1,128]{2,1,0:T(1,128)} %fusion.v_ref), custom_call_target="tpu_custom_call" | custom-call | tf_op jit(solution)/shard_map/inward/pallas_call | solution.py:320
  37.2 59.7 %patch.1 = (bf16[1024,256]{1,0:T(8,128)(2,1)}, bf16[1024,256]{1,0:T(8,128)(2,1)}, bf16[8,80,512]{2,1,0:T(8,128)(2,1)}) custom-call(bf16[1024,256]{1,0:T(8,128)(2,1)} %get-tuple-element.16.x_ref, f32[32,1,128]{2,1,0:T(1,128)} %get-tuple-element.17.v_ref, bf16[1024,256]{1,0:T(8,128)(2,1)} %get-tuple-element.18.g_ref, f32[1,256]{1,0:T(1,128)} %bitcast.3, ...), custom_call_target="tpu_custom_call" | custom-call | tf_op jit(solution)/shard_map/patch/pallas_call | solution.py:337
  96.9 44.6 %outward.1 = (bf16[1024,256]{1,0:T(8,128)(2,1)}, bf16[1024,256]{1,0:T(8,128)(2,1)}, f32[256,768]{1,0:T(8,128)}, f32[256,256]{1,0:T(8,128)}, f32[1,256]{1,0:T(1,128)}) custom-call(bf16[1024,256]{1,0:T(8,128)(2,1)} %get-tuple-element.19.y_ref, bf16[1024,256]{1,0:T(8,128)(2,1)} %get-tuple-element.20.x_ref, bf16[8,80,512]{2,1,0:T(8,128)(2,1)} %get-tuple-element.21.g_ref), custom_call_target="tpu_custom_call" | custom-call | tf_op jit(solution)/shard_map/outward/pallas_call | solution.py:367
  141.5 0.0 copy-start.1
  141.5 0.0 copy-start
  141.5 2.0 %copy.16 = bf16[1024,256]{1,0:T(8,128)(2,1)} copy(bf16[1024,256]{1,0:T(8,128)(2,1)} %get-tuple-element.32) | data formatting | bytes 1048576
  143.5 0.0 copy-done.1
  143.5 0.8 copy.17
  144.3 0.0 copy-done
  144.3 0.0 copy-start.2
  144.3 0.9 copy.18
  145.1 0.2 copy-done.2
  145.4 0.0 copy-start.4
  145.4 0.7 copy.19
  146.1 0.0 copy-done.4
  146.1 0.6 copy.20
  (2 shorter events, 0.0 us)
Async XLA Ops:
  0.6 0.7 copy-start.3
  141.5 2.0 %copy-start.1 = (bf16[1024,256]{1,0:T(8,128)(2,1)S(1)}, bf16[1024,256]{1,0:T(8,128)(2,1)}, u32[]{:S(2)}) copy-start(bf16[1024,256]{1,0:T(8,128)(2,1)} %get-tuple-element.33) | copy-start | bytes 1572868
  141.5 2.8 %copy-start = (f32[256,768]{1,0:T(8,128)S(1)}, f32[256,768]{1,0:T(8,128)}, u32[]{:S(2)}) copy-start(f32[256,768]{1,0:T(8,128)} %get-tuple-element.34) | copy-start | bytes 2359300
  144.3 1.1 copy-start.2
  145.4 0.7 copy-start.4

commit v3 on v2

v3 whole, which is shorter than its diff:
```python
import functools

import jax
import jax.numpy as jnp
from jax import lax
from jax.experimental import pallas as pl
from jax.experimental.pallas import tpu as pltpu
from jax.sharding import PartitionSpec as P

HEADS = 16
K = 1024
MESH = pl.DeviceIdType.MESH
BF = jnp.bfloat16
F32 = jnp.float32
LOG2E = 1.4426950408889634
LIMIT = 56 * 1024 * 1024


def nn(a, b):
    return jnp.dot(a, b, preferred_element_type=F32)


def nt(a, b):
    return lax.dot_general(a, b, (((1,), (1,)), ((), ())), preferred_element_type=F32)


def place(sizes):
    nx, ny = sizes
    n = nx * ny
    me = lax.axis_index("gx") * ny + lax.axis_index("gy")
    return n, ny, me


def enter(sizes):
    n, ny, me = place(sizes)
    barrier = pltpu.get_barrier_semaphore()

    def body(i, c):
        t = lax.rem(me + i, n)
        pl.semaphore_signal(barrier, inc=1, device_id=(t // ny, lax.rem(t, ny)), device_id_type=MESH)
        return c

    lax.fori_loop(1, n, body, 0)
    pl.semaphore_wait(barrier, n - 1)


def exchange(sizes, src, dst, send, recv, one=False):
    n, ny, me = place(sizes)

    def copy(i):
        t = lax.rem(me + i, n)
        return t, pltpu.make_async_remote_copy(
            src_ref=src(t), dst_ref=dst(me), send_sem=send.at[t], recv_sem=recv.at[me],
            device_id=(t // ny, lax.rem(t, ny)), device_id_type=MESH)

    def start(i, c):
        copy(i)[1].start()
        return c

    lax.fori_loop(1, n, start, 0)


def finish(sizes, src, dst, send, recv):
    n, ny, me = place(sizes)

    def wait(i, c):
        t = lax.rem(me + i, n)
        s = lax.rem(me + n - i, n)
        pltpu.make_async_remote_copy(
            src_ref=src(t), dst_ref=dst(s), send_sem=send.at[t], recv_sem=recv.at[s],
            device_id=(t // ny, lax.rem(t, ny)), device_id_type=MESH).wait()
        return c

    lax.fori_loop(1, n, wait, 0)


def rows_of(ref, block):
    return lambda t: ref.at[pl.ds(pl.multiple_of(t * block, block), block), :]


def tile_of(ref):
    return lambda t: ref.at[t]


def parted(left, right, width):
    rows = lax.broadcasted_iota(jnp.int32, (16, 128), 0)
    hi_l, hi_r = left.astype(BF).astype(F32), right.astype(BF).astype(F32)
    block = jnp.where(
        rows == 0, hi_l,
        jnp.where(rows == 1, hi_r,
                  jnp.where(rows == 2, left - hi_l, jnp.where(rows == 3, right - hi_r, 0.0))),
    )
    if width > 128:
        block = jnp.concatenate([block, jnp.zeros((16, width - 128), F32)], 1)
    return block.astype(BF)


def outward_kernel(sizes, root, x_ref, g_ref, xo_ref, gw_ref, gwo_ref, gg_ref,
                   got, half, seen, fine, parts, send, recv, s1, r1, s2, r2, s3, r3):
    nx, ny = sizes
    n, _, me = place(sizes)
    mx, my = lax.axis_index("gx"), lax.axis_index("gy")
    block = x_ref.shape[0] // n
    width = parts.shape[2]
    body = 16 * ny

    def across(size, mine, src, dst, send, recv, along_x):
        for i in range(1, size):
            t = lax.rem(mine + i, size)
            pltpu.make_async_remote_copy(
                src_ref=src(t), dst_ref=dst(mine), send_sem=send.at[t], recv_sem=recv.at[mine],
                device_id=(t, my) if along_x else (mx, t), device_id_type=MESH).start()

    def settle(size, mine, src, dst, send, recv, along_x):
        for i in range(1, size):
            t = lax.rem(mine + i, size)
            s = lax.rem(mine + size - i, size)
            pltpu.make_async_remote_copy(
                src_ref=src(t), dst_ref=dst(s), send_sem=send.at[t], recv_sem=recv.at[s],
                device_id=(t, my) if along_x else (mx, t), device_id_type=MESH).wait()

    first = (nx, mx, tile_of(g_ref), tile_of(got), s1, r1, True)
    second = (ny, my, lambda t: half, tile_of(seen), s2, r2, False)
    third = (nx, mx, lambda t: fine, tile_of(parts), s3, r3, True)
    nodes = (rows_of(x_ref, block), rows_of(xo_ref, block))
    enter(sizes)
    across(*first)
    exchange(sizes, *nodes, send, recv)
    own = pl.ds(pl.multiple_of(me * block, block), block)
    xo_ref[own, :] = x_ref[own, :]
    got[mx] = g_ref[mx]
    settle(*first)
    total = jnp.sum(got[...].astype(F32), 0)
    extra = total[body:, :128]
    half[:body, :] = total[:body].astype(BF)
    half[body:, :] = parted(extra[0:1] + extra[2:3], extra[1:2] + extra[3:4], width)
    across(*second)
    seen[my] = half[...]
    settle(*second)
    total = jnp.sum(seen[...].astype(F32), 0) * root
    fine[...] = total[:body].astype(BF)
    across(*third)
    extra = total[body:, :128]
    gg_ref[:, 0:128] = extra[0:1] + extra[2:3]
    gg_ref[:, 128:256] = extra[1:2] + extra[3:4]
    parts[mx] = fine[...]
    settle(*third)
    side = 1024 // width
    for t in range(n):
        r, c = 16 * (t // side), width * (t % side)
        r0 = 16 * (t % ny)
        left = max(0, min(width, 768 - c))
        if left:
            gw_ref[r : r + 16, c : c + left] = parts[t // ny, r0 : r0 + 16, :left].astype(F32)
        if left < width:
            c0 = c + left - 768
            gwo_ref[r : r + 16, c0 : c0 + width - left] = parts[t // ny, r0 : r0 + 16, left:].astype(F32)
    finish(sizes, *nodes, send, recv)


def split3(a):
    a1 = a.astype(BF)
    rest = a - a1.astype(F32)
    a2 = rest.astype(BF)
    a3 = (rest - a2.astype(F32)).astype(BF)
    return a1, a2, a3


def norm(x_ref):
    x = x_ref[...].astype(F32)
    cent = x - jnp.mean(x, -1, keepdims=True)
    rstd = lax.rsqrt(jnp.mean(cent * cent, -1, keepdims=True) + 1e-05)
    return cent * rstd, rstd


def patch_kernel(sizes, f_ref, v_ref, c_ref, gamma_ref, wqkv_ref, wout_ref,
                 yo_ref, dx_ref, gout_ref,
                 x_ref, vo_ref, g_ref, y_ref, e_ref, ot_ref, inv_ref,
                 qkvt, dot_, attnt, dqkvt, hs, mask, send, recv):
    n, ny, me = place(sizes)
    nx = sizes[0]
    width = wout_ref.shape[0]
    block = f_ref.shape[0] // n
    own = pl.ds(pl.multiple_of(me * block, block), block)
    features = (rows_of(f_ref, block), rows_of(x_ref, block), send.at[0], recv.at[0])
    occupied = (tile_of(v_ref), tile_of(vo_ref), send.at[1], recv.at[1])
    cotangent = (rows_of(c_ref, block), rows_of(g_ref, block), send.at[2], recv.at[2])
    result = (rows_of(y_ref, block), rows_of(yo_ref, block), send.at[3], recv.at[3])
    enter(sizes)
    exchange(sizes, *features)
    exchange(sizes, *occupied)
    x_ref[own, :] = f_ref[own, :]
    vo_ref[me] = v_ref[me]
    g_ref[own, :] = c_ref[own, :]
    finish(sizes, *features)
    finish(sizes, *occupied)
    exchange(sizes, *cotangent)

    gamma = gamma_ref[...]
    hs[...] = (norm(x_ref)[0] * gamma).astype(BF)
    qkvt[...] = nt(wqkv_ref[...].T, hs[...]).astype(BF)
    first = lax.broadcasted_iota(jnp.int32, (16, 128), 0)
    per = n // (K // 128)
    for i in range(K // 128):
        row = vo_ref[per * i]
        for j in range(1, per):
            row = row + vo_ref[per * i + j]
        bias = jnp.where(row > 0.5, 0.0, -1e30)
        mask[:, i * 128 : (i + 1) * 128] = jnp.where(first == 0, bias, 0.0).astype(BF)

    def parts_of(h):
        base = pl.multiple_of(h * 16, 16)
        return (pl.ds(base, 16), pl.ds(pl.multiple_of(width + base, 16), 16),
                pl.ds(pl.multiple_of(2 * width + base, 16), 16))

    def ahead(h, carry):
        at_q, at_k, at_v = parts_of(h)
        kt = qkvt[at_k, :]
        q1, q2, q3 = split3(qkvt[at_q, :].astype(F32) * (0.25 * LOG2E))
        ones = jnp.ones((16, K), BF)
        ka = jnp.concatenate([kt, kt, kt, mask[...]], 0).T
        st = nn(ka, jnp.concatenate([q1, q2, q3, ones], 0))
        e = jnp.exp2(st - jnp.max(st, 0, keepdims=True)).astype(BF)
        e_ref[h] = e
        ot = nn(jnp.concatenate([qkvt[at_v, :], ones], 0), e)
        r = 1.0 / ot[16:17]
        o = ot[:16] * r
        ot_ref[at_q, :] = o
        attnt[at_q, :] = o.astype(BF)
        inv_ref[h] = jnp.broadcast_to(r, (8, K))
        return carry

    lax.fori_loop(0, HEADS, ahead, 0)
    y_ref[...] = (x_ref[...].astype(F32) + nn(attnt[...].T, wout_ref[...])).astype(BF)
    finish(sizes, *cotangent)
    exchange(sizes, *result)
    yo_ref[own, :] = y_ref[own, :]
    dot_[...] = nt(wout_ref[...], g_ref[...]).astype(BF)

    def back(h, carry):
        at_q, at_k, at_v = parts_of(h)
        vt = qkvt[at_v, :]
        rows = lax.broadcasted_iota(jnp.int32, (16, K), 0)
        v2 = jnp.concatenate([vt, vt, jnp.ones((16, K), BF)], 0).T
        e = e_ref[h]
        do = dot_[at_q, :].astype(F32)
        delta = jnp.sum(do * ot_ref[at_q, :], 0, keepdims=True)
        rs = inv_ref[h, 0:1, :] * 0.25
        a = do * rs
        a1 = a.astype(BF)
        a2 = (a - a1.astype(F32)).astype(BF)
        b1, b2, b3 = split3(-delta * rs)
        low = jnp.where(
            rows == 0, b1.astype(F32),
            jnp.where(rows == 1, b2.astype(F32), jnp.where(rows == 2, b3.astype(F32), 0.0)),
        ).astype(BF)
        both = jnp.concatenate([a1, a2], 0)
        dt = nn(v2, jnp.concatenate([both, low], 0))
        ds = (e.astype(F32) * dt).astype(BF)
        dqkvt[at_q, :] = nn(qkvt[at_k, :], ds).astype(BF)
        dqkvt[at_k, :] = nt(qkvt[at_q, :], ds).astype(BF)
        dv = nt(both, e)
        dqkvt[at_v, :] = (4.0 * (dv[:16] + dv[16:])).astype(BF)
        return carry

    lax.fori_loop(0, HEADS, back, 0)

    local_wout = nn(attnt[...], g_ref[...])
    local_wqkv = nn(dqkvt[...], hs[...]).T
    dh = nt(dqkvt[...].T, wqkv_ref[...])
    xhat, rstd = norm(x_ref)
    total = jnp.sum(dh * xhat, 0, keepdims=True)
    g = dh * gamma
    dx = rstd * (g - jnp.mean(g, -1, keepdims=True) - xhat * jnp.mean(g * xhat, -1, keepdims=True))
    dx_ref[...] = (g_ref[...].astype(F32) + dx).astype(BF)
    w = gout_ref.shape[2]
    across = 1024 // w
    extra = parted(total[:, :128], total[:, 128:], w)
    grads = jnp.concatenate([local_wqkv, local_wout], 1).astype(BF)
    for t in range(n):
        r, c = 16 * (t // across), w * (t % across)
        r0 = 16 * (t % ny)
        gout_ref[t // ny, r0 : r0 + 16, :] = grads[r : r + 16, c : c + w]
    for t in range(nx):
        gout_ref[t, 16 * ny :, :] = extra
    finish(sizes, *result)


def shards(sizes, features, valid, cotangent, gamma, w_qkv, w_out):
    n = sizes[0] * sizes[1]
    rows, width = features.shape
    assert rows == K
    block = rows // n
    root = float(rows * n) ** (-0.5)
    me = lax.axis_index("gx") * sizes[1] + lax.axis_index("gy")
    lane = jnp.arange(128, dtype=jnp.int32) // block
    spread = jnp.tile(valid.reshape(n, block), (1, 128 // block))
    spread = jnp.where(lane[None, :] == lax.rem(me, 128 // block), spread, 0).astype(F32)[:, None, :]

    vmem = pl.BlockSpec(memory_space=pltpu.VMEM)
    node = jax.ShapeDtypeStruct((rows, width), BF)
    tile = 16384 // n
    nx, ny = sizes
    y_plain, dx, grads = pl.pallas_call(
        functools.partial(patch_kernel, sizes),
        out_shape=(node, node, jax.ShapeDtypeStruct((nx, 16 * ny + 16, tile), BF)),
        in_specs=[vmem] * 6,
        out_specs=(vmem,) * 3,
        scratch_shapes=[
            pltpu.VMEM((K, width), BF),
            pltpu.VMEM((n, 1, 128), F32),
            pltpu.VMEM((K, width), BF),
            pltpu.VMEM((K, width), BF),
            pltpu.VMEM((HEADS, K, K), BF),
            pltpu.VMEM((width, K), F32),
            pltpu.VMEM((HEADS, 8, K), F32),
            pltpu.VMEM((3 * width, K), BF),
            pltpu.VMEM((width, K), BF),
            pltpu.VMEM((width, K), BF),
            pltpu.VMEM((3 * width, K), BF),
            pltpu.VMEM((K, width), BF),
            pltpu.VMEM((16, K), BF),
            pltpu.SemaphoreType.DMA((4, n)),
            pltpu.SemaphoreType.DMA((4, n)),
        ],
        compiler_params=pltpu.CompilerParams(collective_id=0, has_side_effects=True, vmem_limit_bytes=LIMIT),
        name="patch",
    )(features, spread, cotangent, gamma.reshape(1, width), w_qkv, w_out)

    dx_plain, gw, gwo, gg = pl.pallas_call(
        functools.partial(outward_kernel, sizes, root),
        out_shape=(
            node,
            jax.ShapeDtypeStruct((width, 3 * width), F32),
            jax.ShapeDtypeStruct((width, width), F32),
            jax.ShapeDtypeStruct((1, width), F32),
        ),
        in_specs=[vmem] * 2,
        out_specs=(vmem,) * 4,
        scratch_shapes=[
            pltpu.VMEM((nx, 16 * ny + 16, tile), BF),
            pltpu.VMEM((16 * ny + 16, tile), BF),
            pltpu.VMEM((ny, 16 * ny + 16, tile), BF),
            pltpu.VMEM((16 * ny, tile), BF),
            pltpu.VMEM((nx, 16 * ny, tile), BF),
            pltpu.SemaphoreType.DMA((n,)),
            pltpu.SemaphoreType.DMA((n,)),
        ] + [pltpu.SemaphoreType.DMA((size,)) for size in (nx, nx, ny, ny, nx, nx)],
        compiler_params=pltpu.CompilerParams(collective_id=1, has_side_effects=True, vmem_limit_bytes=LIMIT),
        name="outward",
    )(dx, grads)
    return y_plain, dx_plain, gw, gwo, gg.reshape(width)


def solution(mesh):
    sizes = (mesh.shape["gx"], mesh.shape["gy"])
    both = P(("gx", "gy"), None)
    return jax.shard_map(
        functools.partial(shards, sizes),
        mesh=mesh,
        in_specs=(both, P(("gx", "gy")), both, P(), P(), P()),
        out_specs=(both, both, P(), P(), P()),
        check_vma=False,
    )
```

time: 147 us -> 136 us (0.925)
  Pallas kernels: 139 us -> 128 us
    pallas_call x1, Pallas kernels: 44.6 us -> 34.6 us  [shards(): pl.pallas_call(functools.partial(outward_kernel, sizes, root), out_shape=...]
    pallas_call x2 -> x1, Pallas kernels: 94.7 us -> 93.6 us  [shards(): pl.pallas_call(functools.partial(patch_kernel, sizes), out_shape=(node, n...]
where the time goes in v3:
time: 136 us; the launch traced here: 135 us
  Pallas kernels  128 us (94%)
  local copies, waits for them, and re-layouts  5.89 us (4%)
    pallas_call x1, Pallas kernels, shards(): pl.pallas_call(functools.partial(patch_kernel, sizes), out_shape=(node, n...  93.6 us
    pallas_call x1, Pallas kernels, shards(): pl.pallas_call(functools.partial(outward_kernel, sizes, root), out_shape=...  34.6 us
    unnamed x15, local copies, waits for them, and re-layouts  5.7 us

profile of v3, /device:TPU:0, one launch (start us, length us, event | category | flops | bytes accessed | tf_op | source)
XLA Modules:
  0.0 135.4 jit_solution(11483083495482782075)
XLA Ops:
  0.6 0.0 copy-start.3
  0.7 0.7 copy-done.3
  1.3 0.1 tile.10
  1.4 0.1 tile.12
  1.5 0.6 fusion.v_ref
  2.2 93.6 %patch.1 = (bf16[1024,256]{1,0:T(8,128)(2,1)}, bf16[1024,256]{1,0:T(8,128)(2,1)}, bf16[8,80,512]{2,1,0:T(8,128)(2,1)}) custom-call(bf16[1024,256]{1,0:T(8,128)(2,1)} %f_ref.1, f32[32,1,128]{2,1,0:T(1,128)} %fusion.v_ref, bf16[1024,256]{1,0:T(8,128)(2,1)} %c_ref.1, f32[1,256]{1,0:T(1,128)} %bitcast.3, bf16[256,768]{1,0:T(8,128)(2,1)} %wqkv_ref.1, ...), custom_call_target="tpu_custom_call" | custom-call | tf_op jit(solution)/shard_map/patch/pallas_call | solution.py:304
  95.8 0.0 copy-start.1
  95.8 34.6 %outward.1 = (bf16[1024,256]{1,0:T(8,128)(2,1)}, f32[256,768]{1,0:T(8,128)}, f32[256,256]{1,0:T(8,128)}, f32[1,256]{1,0:T(1,128)}) custom-call(bf16[1024,256]{1,0:T(8,128)(2,1)} %get-tuple-element.13.x_ref, bf16[8,80,512]{2,1,0:T(8,128)(2,1)} %get-tuple-element.14.g_ref), custom_call_target="tpu_custom_call" | custom-call | tf_op jit(solution)/shard_map/outward/pallas_call | solution.py:330
  130.4 0.0 copy-done.1
  130.4 0.0 copy-start
  130.4 0.8 copy.16
  131.2 1.9 %copy.17 = bf16[1024,256]{1,0:T(8,128)(2,1)} copy(bf16[1024,256]{1,0:T(8,128)(2,1)} %get-tuple-element.25) | data formatting | bytes 1048576
  133.1 0.0 copy-done
  133.1 0.0 copy-start.2
  133.1 0.9 copy.18
  133.9 0.2 copy-done.2
  134.1 0.0 copy-start.4
  134.2 0.7 copy.19
  134.9 0.0 copy-done.4
  134.9 0.6 copy.20
  (2 shorter events, 0.0 us)
Async XLA Ops:
  0.6 0.7 copy-start.3
  95.8 34.6 %copy-start.1 = (bf16[1024,256]{1,0:T(8,128)(2,1)S(1)}, bf16[1024,256]{1,0:T(8,128)(2,1)}, u32[]{:S(2)}) copy-start(bf16[1024,256]{1,0:T(8,128)(2,1)} %get-tuple-element.24) | copy-start | bytes 1572868
  130.4 2.7 %copy-start = (f32[256,768]{1,0:T(8,128)S(1)}, f32[256,768]{1,0:T(8,128)}, u32[]{:S(2)}) copy-start(f32[256,768]{1,0:T(8,128)} %get-tuple-element.26) | copy-start | bytes 2359300
  133.1 1.1 copy-start.2
  134.1 0.7 copy-start.4
